TPU v7x, 32 devices: a whole 2x2x4 slice. The times are simulated.
32 devices in a mesh: blk: 8 (over z, x), con: 4 (over y, core).
Axes of the slice: x: 2, y: 2, z: 4, core: 2. Of those that a mesh axis runs over, the one named last changes fastest.
Arguments:
- patch_rows: bfloat16 [4, 1536, 16, 1024], P('con', 'blk'), may hold values from -6 to 6
- subject_ids: int32 [1536], replicated, may hold values from 0 to 383
- logit_scale: float32 [2], replicated, may hold values from 5 to 20
- logit_bias: float32 [2], replicated, may hold values from -6 to -2
Outputs:
- grad_emb: float32 [4, 1536, 1024], P('con', 'blk')
All inputs are finite; a program needn't handle non-finite values.
Results may differ from a plain program's by a relative error of at most 0.0037.
Values may be sent and summed in bfloat16 or wider, within the bound.
A program may use at most 128 MiB of HBM per device.

v0:
```python
import jax
import jax.numpy as jnp
from jax import lax
from jax.sharding import PartitionSpec as P


def from_partner(shard, axis, stride):
    return lax.ppermute(shard, axis, [(i, i ^ 1 << stride) for i in range(lax.axis_size(axis))])


def on_device(patch_rows, subject_ids, logit_scale, logit_bias):
    row_count = patch_rows.shape[1]
    patch_count = patch_rows.shape[2]
    width = patch_rows.shape[3]
    pooled = jnp.sum(patch_rows[0], axis=1, dtype=jnp.float32) / patch_count
    row_norms = jnp.sqrt(jnp.sum(pooled * pooled, axis=1, keepdims=True) + 1e-06)
    own_emb = (pooled / row_norms).astype(jnp.bfloat16)
    contrast = lax.axis_index("con")
    pair_index = contrast // 2
    scale_value = logit_scale[pair_index]
    bias_value = logit_bias[pair_index]
    position = lax.axis_index("blk")
    own_ids = lax.dynamic_slice_in_dim(subject_ids, position * row_count, row_count, 0)
    partner = from_partner(own_emb, "con", 0)
    shard_rows = lax.all_gather(partner, "blk", axis=0, tiled=True)
    logits = (
        scale_value
        * lax.dot_general(
            own_emb, shard_rows, (((1,), (1,)), ((), ())), preferred_element_type=jnp.float32
        )
        + bias_value
    )
    label_sign = jnp.where(own_ids[:, None] == subject_ids[None, :], 1.0, -1.0).astype(jnp.float32)
    coeff = (scale_value * (jax.nn.sigmoid(label_sign * logits) - 1.0) * label_sign).astype(
        jnp.bfloat16
    )
    gradient = jnp.dot(coeff, shard_rows, preferred_element_type=jnp.float32)
    return gradient.reshape(1, row_count, width)


def solution(mesh):
    in_specs = (P("con", "blk", None, None), P(), P(), P())
    out_specs = P("con", "blk", None)
    return jax.shard_map(
        on_device, mesh=mesh, in_specs=in_specs, out_specs=out_specs, check_vma=False
    )
```

profile of v0, /device:TPU:0, one launch (start us, length us, event | category | flops | bytes accessed | tf_op | source)
XLA Modules:
  0.0 92.6 jit_solution(16701474176328392616)
XLA Ops:
  6.5 0.0 all-gather.2.cloned.1.call-start
  6.5 6.1 %convert_reduce_fusion = f32[192,1024]{1,0:T(8,128)S(1)} fusion(bf16[1,192,16,1024]{3,2,1,0:T(8,128)(2,1)} %param.4), kind=kLoop, calls=%fused_computation | loop fusion | flops 6094848 | bytes 7077888 | tf_op jit(solution)/shard_map/reduce_sum | solution.py:15
  12.6 0.0 copy-start.2
  12.6 0.0 copy-start.3
  12.6 0.0 copy-start.1
  12.6 0.2 multiply_reduce_fusion
  12.8 0.1 divide_convert_fusion
  13.0 0.5 collective-permute-start
  13.5 1.3 %collective-permute-done = bf16[192,1024]{1,0:T(8,128)(2,1)S(1)} collective-permute-done((bf16[192,1024]{1,0:T(8,128)(2,1)S(1)}, bf16[192,1024]{1,0:T(8,128)(2,1)S(1)}, u32[]{:S(2)}, u32[]{:S(2)}) %collective-permute-start) | collective-permute-done | bytes 393248 | tf_op jit(solution)/shard_map/ppermute | solution.py:8
  14.8 0.0 copy-start
  14.8 0.7 copy-done
  15.6 0.0 all-gather.2.cloned.1.call-update
  15.6 0.0 copy-done.2
  15.6 0.6 dynamic_slice.11
  16.2 0.0 copy-done.3
  16.2 0.6 dynamic_slice.9
  16.8 0.0 copy-done.1
  16.8 0.1 dynamic_slice.10
  16.9 62.0 %all-gather.2.cloned.1.call-done = bf16[1536,1024]{1,0:T(8,128)(2,1)} async-done(((bf16[192,1024]{1,0:T(8,128)(2,1)}), bf16[1536,1024]{1,0:T(8,128)(2,1)}) %all-gather.2.cloned.1.call-update) | async-done | bytes 3145744 | tf_op jit(solution)/shard_map/all_gather | solution.py:25
  78.8 6.9 %convolution_bitcast_fusion = f32[1,192,1024]{2,1,0:T(8,128)} fusion(bf16[1536,1024]{1,0:T(8,128)(2,1)} %all-gather.2.cloned.1.call-done, bf16[192,1024]{1,0:T(8,128)(2,1)S(1)} %divide_convert_fusion, f32[]{:T(128)} %bitcast.1, s32[1536]{0:T(1024)S(1)} %copy-done.1, f32[]{:T(128)} %bitcast, s32[192]{0:T(256)S(1)} %dynamic_slice.10), kind=kOutput, calls=%fused_computation.12 | convolution fusion | flops 1211498496 | bytes 4332296 | tf_op jit(solution)/shard_map/dot_general | solution.py:37
  (1 shorter events, 0.0 us)
Async XLA Ops:
  6.5 72.3 %all-gather.2.cloned.1.call-start = ((), (), s32[]{:S(2)}) async-start(), calls=%async_computation | async-start | bytes 3538944 | tf_op jit(solution)/shard_map/all_gather | solution.py:25
  12.6 3.0 %copy-start.2 = (f32[2]{0:T(128)S(1)}, f32[2]{0:T(128)}, u32[]{:S(2)}) copy-start(f32[2]{0:T(128)} %param.7) | copy-start | bytes 28
  12.6 3.6 %copy-start.3 = (f32[2]{0:T(128)S(1)}, f32[2]{0:T(128)}, u32[]{:S(2)}) copy-start(f32[2]{0:T(128)} %param.6) | copy-start | bytes 28
  12.6 4.2 %copy-start.1 = (s32[1536]{0:T(1024)S(1)}, s32[1536]{0:T(1024)}, u32[]{:S(2)}) copy-start(s32[1536]{0:T(1024)} %param.5) | copy-start | bytes 18436
  13.0 1.9 %collective-permute-start = (bf16[192,1024]{1,0:T(8,128)(2,1)S(1)}, bf16[192,1024]{1,0:T(8,128)(2,1)S(1)}, u32[]{:S(2)}, u32[]{:S(2)}) collective-permute-start(bf16[192,1024]{1,0:T(8,128)(2,1)S(1)} %divide_convert_fusion), channel_id=1, source_target_pairs={{0,1},{1,0},{2,3},{3,2},{4,5},{5,4},{6,7},{7,6},{8,9},{9,8},{10,11... | collective-permute-start | bytes 1179656 | tf_op jit(solution)/shard_map/ppermute | solution.py:8
  14.8 0.7 copy-start
Sparse Core Ops, SparseCore 0:
  15.7 63.0 all-gather.1
where the time goes:
time: 92.7 us; the launch traced here: 92.6 us
  waiting for transfers between devices  63.3 us (68%)
  between operations  13.5 us (15%)
  matrix products  6.9 us (7%)
  other arithmetic  6.38 us (7%)
  local copies, waits for them, and re-layouts  1.99 us (2%)
    all_gather x1, waiting for transfers between devices, on_device(): shard_rows = lax.all_gather(partner, 'blk', axis=0, tiled=True)  62 us
    dot_general x1, matrix products, on_device(): gradient = jnp.dot(coeff, shard_rows, preferred_element_type=jnp.float32)  6.9 us
    reduce_sum x1, other arithmetic, on_device(): pooled = jnp.sum(patch_rows[0], axis=1, dtype=jnp.float32) / patch_count  6.06 us
  transfers between devices with their start and end apart: 2, of which 2 were waited for; matrix products, arithmetic and copies ran while one was open for 1% of the time, Pallas kernels for 0%

commit v1 on v0

v1 whole, which is shorter than its diff:
```python
import functools
import jax
import jax.numpy as jnp
from jax import lax
from jax.experimental import pallas as pl
from jax.experimental.pallas import tpu as pltpu
from jax.sharding import PartitionSpec as P

MESH = pl.DeviceIdType.MESH


def kernel(n, fast, scale_ref, bias_ref, ids_ref, x_ref, out_ref, xbuf, own, blocks, ids_col,
           in_sem, swap_sem, recv_sem, up_sem, down_sem, cross_sem):
    rows, patches, width = x_ref.shape[1:]
    slow = n // fast
    con = lax.axis_index("con")
    pos = lax.axis_index("blk")
    z = pos // fast
    x = pos % fast
    pair = con // 2
    partner = con + 1 - 2 * (con % 2)
    across = x + 1 - 2 * (x % 2)
    group = 16
    steps = xbuf.shape[0]
    chunk = rows // steps

    def load(i):
        return pltpu.make_async_copy(
            x_ref.at[0, pl.ds(i * chunk, chunk)], xbuf.at[i], in_sem.at[i])

    for i in range(steps):
        load(i).start()

    barrier = pltpu.get_barrier_semaphore()
    pl.semaphore_signal(barrier, inc=1, device_id=(pos, partner), device_id_type=MESH)
    pl.semaphore_signal(barrier, inc=1, device_id=(z * fast + across, con), device_id_type=MESH)

    @pl.when(z > 0)
    def _():
        pl.semaphore_signal(barrier, inc=1, device_id=(pos - fast, con), device_id_type=MESH)

    @pl.when(z < slow - 1)
    def _():
        pl.semaphore_signal(barrier, inc=1, device_id=(pos + fast, con), device_id_type=MESH)

    mine = ids_ref[pl.ds(pos, 1), :].astype(jnp.float32)
    eye = (lax.broadcasted_iota(jnp.int32, (rows, rows), 0)
           == lax.broadcasted_iota(jnp.int32, (rows, rows), 1))
    ids_col[...] = jnp.sum(jnp.where(eye, mine, 0.0), axis=1, keepdims=True)

    ones = (lax.broadcasted_iota(jnp.int32, (group, group * patches), 1) // patches
            == lax.broadcasted_iota(jnp.int32, (group, group * patches), 0)).astype(jnp.bfloat16)
    for i in range(steps):
        load(i).wait()
        for g in range(chunk // group):
            tile = xbuf[i, pl.ds(g * group, group)].reshape(group * patches, width)
            pooled = jnp.dot(ones, tile, preferred_element_type=jnp.float32) * (1.0 / patches)
            norm = lax.rsqrt(jnp.sum(pooled * pooled, axis=1, keepdims=True) + 1e-6)
            own[pl.ds(i * chunk + g * group, group), :] = (pooled * norm).astype(jnp.bfloat16)

    pl.semaphore_wait(barrier, 2 + jnp.where(z > 0, 1, 0) + jnp.where(z < slow - 1, 1, 0))

    swap = pltpu.make_async_remote_copy(
        src_ref=own, dst_ref=blocks.at[pos], send_sem=swap_sem, recv_sem=recv_sem.at[pos],
        device_id=(pos, partner), device_id_type=MESH)
    swap.start()

    def send(slot, target, sem):
        return pltpu.make_async_remote_copy(
            src_ref=blocks.at[slot], dst_ref=blocks.at[slot], send_sem=sem.at[slot // fast],
            recv_sem=recv_sem.at[slot], device_id=(target, con), device_id_type=MESH)

    def arrived(slot):
        pltpu.make_async_remote_copy(
            src_ref=blocks.at[slot], dst_ref=blocks.at[slot], send_sem=swap_sem,
            recv_sem=recv_sem.at[slot], device_id=(pos, partner), device_id_type=MESH).wait_recv()

    near = jnp.minimum(z, slow - 1 - z)
    far_sign = jnp.where(z < slow - 1 - z, 1, -1)

    def layer(k):
        both = ((k + 1) // 2) * jnp.where(k % 2 == 1, 1, -1)
        return z + jnp.where(k <= 2 * near, both, far_sign * (k - near))

    scale = scale_ref[pair]
    bias = bias_ref[pair]

    def add_block(slot, first):
        block = blocks[slot]
        dots = lax.dot_general(own[...], block, (((1,), (1,)), ((), ())),
                               preferred_element_type=jnp.float32)
        logits = scale * dots + bias
        same = ids_col[...] == ids_ref[pl.ds(slot, 1), :].astype(jnp.float32)
        sign = jnp.where(same, 1.0, -1.0)
        coeff = ((-scale * sign) / (1.0 + jnp.exp(sign * logits))).astype(jnp.bfloat16)
        grad = jnp.dot(coeff, block, preferred_element_type=jnp.float32)
        if first:
            out_ref[0] = grad
        else:
            out_ref[0] += grad

    def relay(k):
        zz = layer(k)
        slot = zz * fast + x
        arrived(slot)

        @pl.when((z < slow - 1) & (zz <= z))
        def _():
            send(slot, pos + fast, up_sem).start()

        @pl.when((z > 0) & (zz >= z))
        def _():
            send(slot, pos - fast, down_sem).start()

        send(slot, z * fast + across, cross_sem).start()
        return slot

    add_block(relay(0), True)

    def own_line(k, carry):
        add_block(relay(k), False)
        return carry

    lax.fori_loop(1, slow, own_line, 0)

    def other_line(k, carry):
        slot = layer(k) * fast + across
        arrived(slot)
        add_block(slot, False)
        return carry

    lax.fori_loop(0, slow, other_line, 0)

    swap.wait_send()

    def drain(zz, carry):
        slot = zz * fast + x

        @pl.when((z < slow - 1) & (zz <= z))
        def _():
            send(slot, pos + fast, up_sem).wait_send()

        @pl.when((z > 0) & (zz >= z))
        def _():
            send(slot, pos - fast, down_sem).wait_send()

        send(slot, z * fast + across, cross_sem).wait_send()
        return carry

    lax.fori_loop(0, slow, drain, 0)


def solution(mesh):
    n = mesh.shape["blk"]
    fast = 2
    slow = n // fast

    def on_device(patch_rows, subject_ids, logit_scale, logit_bias):
        _, rows, patches, width = patch_rows.shape
        chunk = 48 if rows % 48 == 0 else rows
        return pl.pallas_call(
            functools.partial(kernel, n, fast),
            out_shape=jax.ShapeDtypeStruct((1, rows, width), jnp.float32),
            in_specs=[pl.BlockSpec(memory_space=pltpu.SMEM), pl.BlockSpec(memory_space=pltpu.SMEM),
                      pl.BlockSpec(memory_space=pltpu.VMEM), pl.BlockSpec(memory_space=pl.ANY)],
            out_specs=pl.BlockSpec(memory_space=pltpu.VMEM),
            scratch_shapes=[
                pltpu.VMEM((rows // chunk, chunk, patches, width), jnp.bfloat16),
                pltpu.VMEM((rows, width), jnp.bfloat16),
                pltpu.VMEM((n, rows, width), jnp.bfloat16),
                pltpu.VMEM((rows, 1), jnp.float32),
                pltpu.SemaphoreType.DMA((rows // chunk,)),
                pltpu.SemaphoreType.DMA,
                pltpu.SemaphoreType.DMA((n,)),
                pltpu.SemaphoreType.DMA((slow,)),
                pltpu.SemaphoreType.DMA((slow,)),
                pltpu.SemaphoreType.DMA((slow,)),
            ],
            compiler_params=pltpu.CompilerParams(
                collective_id=0, has_side_effects=True, vmem_limit_bytes=52 * 2**20),
        )(logit_scale, logit_bias, subject_ids.reshape(n, rows), patch_rows)

    return jax.shard_map(
        on_device, mesh=mesh, in_specs=(P("con", "blk", None, None), P(), P(), P()),
        out_specs=P("con", "blk", None), check_vma=False)
```

time: 92.7 us -> 53.1 us (0.57)
  waiting for transfers between devices: 63.3 us -> 0 us
  Pallas kernels: 0 us -> 49.9 us
  between operations: 13.5 us -> 0.01 us
  matrix products: 6.9 us -> 0 us
  other arithmetic: 6.38 us -> 0 us
  local copies, waits for them, and re-layouts: 1.99 us -> 2.96 us
    all_gather x1 -> x0, waiting for transfers between devices: 62 us -> none  [on_device(): shard_rows = lax.all_gather(partner, 'blk', axis=0, tiled=True)]
    pallas_call x0 -> x1, Pallas kernels: none -> 49.9 us  [on_device(): pl.pallas_call(functools.partial(kernel, n, fast), out_shape=jax.ShapeDty...]
    dot_general x1 -> x0, matrix products: 6.9 us -> none  [on_device(): gradient = jnp.dot(coeff, shard_rows, preferred_element_type=jnp.float32)]
    reduce_sum x2 -> x0, other arithmetic: 6.22 us -> none  [the longest x1 6.06 us: on_device(): pooled = jnp.sum(patch_rows[0], axis=1, dtype=jnp.float32) / patch_count]
    unnamed x8 -> x5, local copies, waits for them, and re-layouts: 0.76 us -> 2.19 us
    ppermute x1 -> x0, waiting for transfers between devices: 1.35 us -> none  [from_partner(): lax.ppermute(shard, axis, [(i, i ^ 1 << stride) for i in range(lax.axis_s...]
    dynamic_slice x3 -> x0, local copies, waits for them, and re-layouts: 1.22 us -> none  [the longest x1 0.59 us: on_device(): bias_value = logit_bias[pair_index]]
  transfers between devices with their start and end apart: 2 -> 0, of which waited for: 2 -> 0; matrix products, arithmetic and copies ran while one was open for 1% -> 0% of each run, Pallas kernels for 0% -> 0%
where the time goes in v1:
time: 53.1 us; the launch traced here: 52.9 us
  Pallas kernels  49.9 us (94%)
  local copies, waits for them, and re-layouts  2.96 us (6%)
    pallas_call x1, Pallas kernels, on_device(): pl.pallas_call(functools.partial(kernel, n, fast), out_shape=jax.ShapeDty...  49.9 us
    unnamed x5, local copies, waits for them, and re-layouts  2.19 us

profile of v1, /device:TPU:0, one launch (start us, length us, event | category | flops | bytes accessed | tf_op | source)
XLA Modules:
  0.0 52.9 jit_solution(11828293700260534599)
XLA Ops:
  0.0 0.8 %reshape.3.ids_ref = s32[8,192]{1,0:T(8,128)S(1)} reshape(s32[1536]{0:T(1024)} %param.5) | data formatting | bytes 12288 | tf_op jit(solution)/shard_map/reshape | solution.py:181
  0.8 0.0 copy-start
  0.8 0.7 %copy-done = f32[2]{0:T(128)S(1)} copy-done((f32[2]{0:T(128)S(1)}, f32[2]{0:T(128)}, u32[]{:S(2)}) %copy-start) | copy-done | bytes 32
  1.4 0.0 copy-start.1
  1.4 0.7 %copy-done.1 = f32[2]{0:T(128)S(1)} copy-done((f32[2]{0:T(128)S(1)}, f32[2]{0:T(128)}, u32[]{:S(2)}) %copy-start.1) | copy-done | bytes 32
  2.1 49.9 %shard_map.46 = f32[1,192,1024]{2,1,0:T(8,128)S(1)} custom-call(f32[2]{0:T(128)S(1)} %copy-done, f32[2]{0:T(128)S(1)} %copy-done.1, s32[8,192]{1,0:T(8,128)S(1)} %reshape.3.ids_ref, bf16[1,192,16,1024]{3,2,1,0:T(8,128)(2,1)} %x_ref.1), custom_call_target="tpu_custom_call" | custom-call | tf_op jit(solution)/shard_map/pallas_call | solution.py:161
  52.0 0.9 %copy.6 = f32[1,192,1024]{2,1,0:T(8,128)} copy(f32[1,192,1024]{2,1,0:T(8,128)S(1)} %shard_map.46) | data formatting | bytes 1572864
Async XLA Ops:
  0.8 0.7 %copy-start = (f32[2]{0:T(128)S(1)}, f32[2]{0:T(128)}, u32[]{:S(2)}) copy-start(f32[2]{0:T(128)} %scale_ref.1) | copy-start | bytes 28
  1.4 0.7 %copy-start.1 = (f32[2]{0:T(128)S(1)}, f32[2]{0:T(128)}, u32[]{:S(2)}) copy-start(f32[2]{0:T(128)} %bias_ref.1) | copy-start | bytes 28

commit v2 on v1

v2 whole, which is shorter than its diff:
```python
import functools
import jax
import jax.numpy as jnp
from jax import lax
from jax.experimental import pallas as pl
from jax.experimental.pallas import tpu as pltpu
from jax.sharding import PartitionSpec as P

MESH = pl.DeviceIdType.MESH


def kernel(n, fast, scale_ref, bias_ref, ids_ref, x_ref, out_ref, xbuf, own, a_rows, b_rows,
           ids_col, part, acc_b, rs_out, rs_up, rs_down, b_half_out, b_half_in, b_cross_out,
           b_cross_in, last_out, last_in, in_sem, swap_send, swap_recv, a_recv, up_send, down_send,
           b_cross_send, b_cross_recv, b_relay_send, b_relay_recv, rs_send, up_recv, down_recv,
           gb_send, gb_recv):
    rows, patches, width = x_ref.shape[1:]
    half = rows // 2
    slow = n // fast
    con = lax.axis_index("con")
    pos = lax.axis_index("blk")
    z = pos // fast
    x = pos % fast
    pair = con // 2
    core = con % 2
    partner = con + 1 - 2 * core
    across = x + 1 - 2 * (x % 2)
    group = 16
    steps = xbuf.shape[0]
    chunk = rows // steps
    on_chip = dict(device_id=(pos, partner), device_id_type=MESH)
    on_cross = dict(device_id=(z * fast + across, con), device_id_type=MESH)
    on_up = dict(device_id=(pos + fast, con), device_id_type=MESH)
    on_down = dict(device_id=(pos - fast, con), device_id_type=MESH)
    has_up = z < slow - 1
    has_down = z > 0

    def load(i):
        return pltpu.make_async_copy(
            x_ref.at[0, pl.ds(i * chunk, chunk)], xbuf.at[i], in_sem.at[i])

    for i in range(steps):
        load(i).start()

    barrier = pltpu.get_barrier_semaphore()
    pl.semaphore_signal(barrier, inc=1, **on_chip)
    pl.semaphore_signal(barrier, inc=1, **on_cross)

    @pl.when(has_down)
    def _():
        pl.semaphore_signal(barrier, inc=1, **on_down)

    @pl.when(has_up)
    def _():
        pl.semaphore_signal(barrier, inc=1, **on_up)

    eye = (lax.broadcasted_iota(jnp.int32, (rows, rows), 0)
           == lax.broadcasted_iota(jnp.int32, (rows, rows), 1))

    def column(zz, carry):
        line = ids_ref[pl.ds(zz * fast + x, 1), :].astype(jnp.float32)
        ids_col[zz] = jnp.sum(jnp.where(eye, line, 0.0), axis=1, keepdims=True)
        return carry

    lax.fori_loop(0, slow, column, 0)

    ones = (lax.broadcasted_iota(jnp.int32, (group, group * patches), 1) // patches
            == lax.broadcasted_iota(jnp.int32, (group, group * patches), 0)).astype(jnp.bfloat16)
    for i in range(steps):
        load(i).wait()
        for g in range(chunk // group):
            tile = xbuf[i, pl.ds(g * group, group)].reshape(group * patches, width)
            pooled = jnp.dot(ones, tile, preferred_element_type=jnp.float32) * (1.0 / patches)
            norm = lax.rsqrt(jnp.sum(pooled * pooled, axis=1, keepdims=True) + 1e-6)
            at = i * chunk + g * group
            own[at // half, pl.ds(at % half, group), :] = (pooled * norm).astype(jnp.bfloat16)

    pl.semaphore_wait(barrier, 2 + jnp.where(has_down, 1, 0) + jnp.where(has_up, 1, 0))

    a_swap = pltpu.make_async_remote_copy(
        src_ref=own.at[1], dst_ref=a_rows.at[z], send_sem=swap_send, recv_sem=a_recv.at[z], **on_chip)
    b_swap = pltpu.make_async_remote_copy(
        src_ref=own, dst_ref=b_rows.at[x], send_sem=swap_send, recv_sem=swap_recv, **on_chip)
    b_cross = pltpu.make_async_remote_copy(
        src_ref=b_rows.at[x, core], dst_ref=b_rows.at[x, core], send_sem=b_cross_send,
        recv_sem=b_cross_recv, **on_cross)
    b_cross_arrival = pltpu.make_async_remote_copy(
        src_ref=b_rows.at[across, core], dst_ref=b_rows.at[across, core], send_sem=b_cross_send,
        recv_sem=b_cross_recv, **on_cross)
    b_relay = pltpu.make_async_remote_copy(
        src_ref=b_rows.at[across, core], dst_ref=b_rows.at[across, core], send_sem=b_relay_send,
        recv_sem=b_relay_recv, **on_chip)
    b_relay_arrival = pltpu.make_async_remote_copy(
        src_ref=b_rows.at[across, 1 - core], dst_ref=b_rows.at[across, 1 - core],
        send_sem=b_relay_send, recv_sem=b_relay_recv, **on_chip)

    def a_up(zz):
        return pltpu.make_async_remote_copy(
            src_ref=a_rows.at[zz], dst_ref=a_rows.at[zz], send_sem=up_send.at[zz],
            recv_sem=a_recv.at[zz], **on_up)

    def a_down(zz):
        return pltpu.make_async_remote_copy(
            src_ref=a_rows.at[zz], dst_ref=a_rows.at[zz], send_sem=down_send.at[zz],
            recv_sem=a_recv.at[zz], **on_down)

    def forward(zz):
        @pl.when(has_up & (zz <= z))
        def _():
            a_up(zz).start()

        @pl.when(has_down & (zz >= z))
        def _():
            a_down(zz).start()

    @pl.when(core == 0)
    def _():
        a_rows[z] = own[0]
        a_swap.start()
        forward(z)
        b_swap.wait_recv()
        b_cross.start()

    @pl.when(core == 1)
    def _():
        b_rows[x] = own[...]
        b_swap.start()
        b_cross.start()
        a_swap.wait_recv()
        forward(z)

    near = jnp.minimum(z, slow - 1 - z)
    far_sign = jnp.where(z < slow - 1 - z, 1, -1)

    def layer(k):
        both = ((k + 1) // 2) * jnp.where(k % 2 == 1, 1, -1)
        return z + jnp.where(k <= 2 * near, both, far_sign * (k - near))

    scale = scale_ref[pair]
    bias = bias_ref[pair]

    def block(zz, xx, first):
        rows_a = a_rows[zz]
        rows_b = b_rows[xx].reshape(rows, width)
        dots = lax.dot_general(rows_a, rows_b, (((1,), (1,)), ((), ())),
                               preferred_element_type=jnp.float32)
        logits = scale * dots + bias
        labels = ids_col[zz, pl.ds(pl.multiple_of(core * half, 16), half), :]
        same = labels == ids_ref[pl.ds(z * fast + xx, 1), :].astype(jnp.float32)
        sign = jnp.where(same, 1.0, -1.0)
        coeff = ((-scale * sign) / (1.0 + jnp.exp(sign * logits))).astype(jnp.bfloat16)
        grad_b = lax.dot_general(coeff, rows_a, (((0,), (0,)), ((), ())),
                                 preferred_element_type=jnp.float32).reshape(2, half, width)
        if first:
            acc_b[xx] = grad_b
        else:
            acc_b[xx] += grad_b
        return jnp.dot(coeff, rows_b, preferred_element_type=jnp.float32)

    def rs_to_up(d):
        return pltpu.make_async_remote_copy(
            src_ref=rs_out.at[d], dst_ref=rs_up.at[d], send_sem=rs_send.at[d],
            recv_sem=up_recv.at[d], **on_up)

    def rs_to_down(d):
        return pltpu.make_async_remote_copy(
            src_ref=rs_out.at[d], dst_ref=rs_down.at[d], send_sem=rs_send.at[d],
            recv_sem=down_recv.at[d], **on_down)

    def compute(zz):
        part[zz] = block(zz, x, False)
        part[zz] += block(zz, across, False)

        @pl.when((z == 0) & (zz > z))
        def _():
            rs_out[zz] = part[zz].astype(jnp.bfloat16)
            rs_to_up(zz).start()

        @pl.when((z == slow - 1) & (zz < z))
        def _():
            rs_out[zz] = part[zz].astype(jnp.bfloat16)
            rs_to_down(zz).start()

    def relay(k):
        zz = layer(k)
        a_up(zz).wait_recv()
        forward(zz)
        return zz

    part[z] = block(z, x, True)
    if slow > 1:
        second = relay(1)
    b_cross_arrival.wait_recv()
    b_relay.start()
    b_relay_arrival.wait_recv()
    part[z] += block(z, across, True)
    if slow > 1:
        compute(second)

    def line(k, carry):
        compute(relay(k))
        return carry

    lax.fori_loop(2, slow, line, 0)

    b_half = pltpu.make_async_remote_copy(
        src_ref=b_half_out, dst_ref=b_half_in, send_sem=gb_send.at[0], recv_sem=gb_recv.at[0], **on_chip)
    b_sum = pltpu.make_async_remote_copy(
        src_ref=b_cross_out, dst_ref=b_cross_in, send_sem=gb_send.at[1], recv_sem=gb_recv.at[1], **on_cross)
    b_half_out[...] = acc_b[across, 1 - core].astype(jnp.bfloat16)
    b_half.start()
    b_half.wait_recv()
    b_cross_out[...] = (acc_b[across, core] + b_half_in[...].astype(jnp.float32)).astype(jnp.bfloat16)
    b_sum.start()

    def pass_on(t, carry):
        @pl.when(has_down & (t > 2 * z) & (t < slow + z))
        def _():
            d = t - z
            rs_to_up(d).wait_recv()
            rs_out[d] = (part[d] + rs_up[d].astype(jnp.float32)).astype(jnp.bfloat16)
            rs_to_up(d).start()

        z_back = slow - 1 - z

        @pl.when(has_up & (t > 2 * z_back) & (t < slow + z_back))
        def _():
            d = slow - 1 - (t - z_back)
            rs_to_down(d).wait_recv()
            rs_out[d] = (part[d] + rs_down[d].astype(jnp.float32)).astype(jnp.bfloat16)
            rs_to_down(d).start()

        return carry

    lax.fori_loop(3, 2 * slow - 2, pass_on, 0)

    b_sum.wait_recv()
    to_b = pltpu.make_async_remote_copy(
        src_ref=last_out, dst_ref=last_in, send_sem=gb_send.at[2], recv_sem=gb_recv.at[2], **on_chip)
    to_a = pltpu.make_async_remote_copy(
        src_ref=last_out.at[0], dst_ref=last_in.at[0], send_sem=gb_send.at[2], recv_sem=gb_recv.at[2],
        **on_chip)

    @pl.when(core == 0)
    def _():
        last_out[0] = (acc_b[x, 0] + b_cross_in[...].astype(jnp.float32)).astype(jnp.bfloat16)
        last_out[1] = acc_b[x, 1].astype(jnp.bfloat16)
        to_b.start()

    @pl.when(has_down)
    def _():
        rs_to_up(z).wait_recv()
        part[z] += rs_up[z].astype(jnp.float32)

    @pl.when(has_up)
    def _():
        rs_to_down(z).wait_recv()
        part[z] += rs_down[z].astype(jnp.float32)

    @pl.when(core == 0)
    def _():
        out_ref[0, pl.ds(0, half), :] = part[z]
        to_a.wait_recv()
        out_ref[0, pl.ds(half, half), :] = last_in[0].astype(jnp.float32)
        a_swap.wait_send()
        to_b.wait_send()

    @pl.when(core == 1)
    def _():
        last_out[0] = part[z].astype(jnp.bfloat16)
        to_a.start()
        to_b.wait_recv()
        out_ref[0, pl.ds(0, half), :] = acc_b[x, 0] + last_in[0].astype(jnp.float32)
        out_ref[0, pl.ds(half, half), :] = (
            acc_b[x, 1] + last_in[1].astype(jnp.float32) + b_cross_in[...].astype(jnp.float32))
        b_swap.wait_send()
        to_a.wait_send()

    b_cross.wait_send()
    b_relay.wait_send()
    b_half.wait_send()
    b_sum.wait_send()

    def drain(zz, carry):
        @pl.when(has_up & (zz <= z))
        def _():
            a_up(zz).wait_send()

        @pl.when(has_down & (zz >= z))
        def _():
            a_down(zz).wait_send()

        @pl.when(zz > z)
        def _():
            rs_to_up(zz).wait_send()

        @pl.when(zz < z)
        def _():
            rs_to_down(zz).wait_send()

        return carry

    lax.fori_loop(0, slow, drain, 0)


def solution(mesh):
    n = mesh.shape["blk"]
    fast = 2
    slow = n // fast

    def on_device(patch_rows, subject_ids, logit_scale, logit_bias):
        _, rows, patches, width = patch_rows.shape
        half = rows // 2
        chunk = 48 if rows % 48 == 0 else rows
        bf16, f32 = jnp.bfloat16, jnp.float32
        dma = pltpu.SemaphoreType.DMA
        return pl.pallas_call(
            functools.partial(kernel, n, fast),
            out_shape=jax.ShapeDtypeStruct((1, rows, width), jnp.float32),
            in_specs=[pl.BlockSpec(memory_space=pltpu.SMEM), pl.BlockSpec(memory_space=pltpu.SMEM),
                      pl.BlockSpec(memory_space=pltpu.VMEM), pl.BlockSpec(memory_space=pl.ANY)],
            out_specs=pl.BlockSpec(memory_space=pltpu.VMEM),
            scratch_shapes=[
                pltpu.VMEM((rows // chunk, chunk, patches, width), bf16),
                pltpu.VMEM((2, half, width), bf16),
                pltpu.VMEM((slow, half, width), bf16),
                pltpu.VMEM((fast, 2, half, width), bf16),
                pltpu.VMEM((slow, rows, 1), f32),
                pltpu.VMEM((slow, half, width), f32),
                pltpu.VMEM((fast, 2, half, width), f32),
                pltpu.VMEM((slow, half, width), bf16),
                pltpu.VMEM((slow, half, width), bf16),
                pltpu.VMEM((slow, half, width), bf16),
                pltpu.VMEM((half, width), bf16),
                pltpu.VMEM((half, width), bf16),
                pltpu.VMEM((half, width), bf16),
                pltpu.VMEM((half, width), bf16),
                pltpu.VMEM((2, half, width), bf16),
                pltpu.VMEM((2, half, width), bf16),
                dma((rows // chunk,)), dma, dma, dma((slow,)), dma((slow,)), dma((slow,)),
                dma, dma, dma, dma, dma((slow,)), dma((slow,)), dma((slow,)), dma((3,)), dma((3,)),
            ],
            compiler_params=pltpu.CompilerParams(
                collective_id=0, has_side_effects=True, vmem_limit_bytes=60 * 2**20),
        )(logit_scale, logit_bias, subject_ids.reshape(n, rows), patch_rows)

    return jax.shard_map(
        on_device, mesh=mesh, in_specs=(P("con", "blk", None, None), P(), P(), P()),
        out_specs=P("con", "blk", None), check_vma=False)
```

time: 53.1 us -> 48.2 us (0.908)
  Pallas kernels: 49.9 us -> 44.5 us
    pallas_call x1, Pallas kernels: 49.9 us -> 44.5 us  [on_device(): pl.pallas_call(functools.partial(kernel, n, fast), out_shape=jax.ShapeDty...]
    reshape x1, local copies, waits for them, and re-layouts: 0.77 us -> 1.36 us  [on_device(): subject_ids.reshape(n, rows)]
    unnamed x5 -> x1, local copies, waits for them, and re-layouts: 2.19 us -> 2.09 us
where the time goes in v2:
time: 48.2 us; the launch traced here: 47.9 us
  Pallas kernels  44.5 us (92%)
  local copies, waits for them, and re-layouts  3.45 us (7%)
    pallas_call x1, Pallas kernels, on_device(): pl.pallas_call(functools.partial(kernel, n, fast), out_shape=jax.ShapeDty...  44.5 us
    unnamed x1, local copies, waits for them, and re-layouts  2.09 us
    reshape x1, local copies, waits for them, and re-layouts, on_device(): subject_ids.reshape(n, rows)  1.36 us

profile of v2, /device:TPU:0, one launch (start us, length us, event | category | flops | bytes accessed | tf_op | source)
XLA Modules:
  0.0 47.9 jit_solution(7286155024382354571)
XLA Ops:
  0.0 1.4 %reshape.3.ids_ref = s32[8,192]{1,0:T(8,128)} reshape(s32[1536]{0:T(1024)} %param.5) | data formatting | bytes 12288 | tf_op jit(solution)/shard_map/reshape | solution.py:345
  1.4 44.5 %shard_map.46 = f32[1,192,1024]{2,1,0:T(8,128)} custom-call(f32[2]{0:T(128)} %scale_ref.1, f32[2]{0:T(128)} %bias_ref.1, s32[8,192]{1,0:T(8,128)} %reshape.3.ids_ref, bf16[1,192,16,1024]{3,2,1,0:T(8,128)(2,1)} %x_ref.1), custom_call_target="tpu_custom_call" | custom-call | tf_op jit(solution)/shard_map/pallas_call | solution.py:317
  45.8 2.1 %copy.6 = f32[1,192,1024]{2,1,0:T(8,128)} copy(f32[1,192,1024]{2,1,0:T(8,128)} %shard_map.46) | data formatting | bytes 1572864

commit v3 on v2

--- a/solution.py
+++ b/solution.py
@@ -190,6 +190,11 @@
     part[z] = block(z, x, True)
     if slow > 1:
         second = relay(1)
+    if slow > 2:
+        @pl.when(near >= 1)
+        def _():
+            relay(2)
+
     b_cross_arrival.wait_recv()
     b_relay.start()
     b_relay_arrival.wait_recv()
@@ -198,7 +203,11 @@
         compute(second)
 
     def line(k, carry):
-        compute(relay(k))
+        @pl.when((k != 2) | (near < 1))
+        def _():
+            relay(k)
+
+        compute(layer(k))
         return carry
 
     lax.fori_loop(2, slow, line, 0)

time: 48.2 us -> 46.9 us (0.973)
  Pallas kernels: 44.5 us -> 43.1 us
    pallas_call x1, Pallas kernels: 44.5 us -> 43.1 us  [on_device(): pl.pallas_call(functools.partial(kernel, n, fast), out_shape=jax.ShapeDty...]
where the time goes in v3:
time: 46.9 us; the launch traced here: 46.6 us
  Pallas kernels  43.1 us (92%)
  local copies, waits for them, and re-layouts  3.45 us (7%)
    pallas_call x1, Pallas kernels, on_device(): pl.pallas_call(functools.partial(kernel, n, fast), out_shape=jax.ShapeDty...  43.1 us
    unnamed x1, local copies, waits for them, and re-layouts  2.09 us
    reshape x1, local copies, waits for them, and re-layouts, on_device(): subject_ids.reshape(n, rows)  1.36 us

profile of v3, /device:TPU:0, one launch (start us, length us, event | category | flops | bytes accessed | tf_op | source)
XLA Modules:
  0.0 46.6 jit_solution(2191645176237120319)
XLA Ops:
  0.0 1.4 %reshape.3.ids_ref = s32[8,192]{1,0:T(8,128)} reshape(s32[1536]{0:T(1024)} %param.5) | data formatting | bytes 12288 | tf_op jit(solution)/shard_map/reshape | solution.py:354
  1.4 43.1 %shard_map.46 = f32[1,192,1024]{2,1,0:T(8,128)} custom-call(f32[2]{0:T(128)} %scale_ref.1, f32[2]{0:T(128)} %bias_ref.1, s32[8,192]{1,0:T(8,128)} %reshape.3.ids_ref, bf16[1,192,16,1024]{3,2,1,0:T(8,128)(2,1)} %x_ref.1), custom_call_target="tpu_custom_call" | custom-call | tf_op jit(solution)/shard_map/pallas_call | solution.py:326
  44.5 2.1 %copy.6 = f32[1,192,1024]{2,1,0:T(8,128)} copy(f32[1,192,1024]{2,1,0:T(8,128)} %shard_map.46) | data formatting | bytes 1572864

commit v4 on v3

--- a/solution.py
+++ b/solution.py
@@ -323,6 +323,8 @@
         chunk = 48 if rows % 48 == 0 else rows
         bf16, f32 = jnp.bfloat16, jnp.float32
         dma = pltpu.SemaphoreType.DMA
+        need = 2 * rows * patches * width + half * width * (12 * slow + 12 * fast + 28)
+        need += slow * rows * 512
         return pl.pallas_call(
             functools.partial(kernel, n, fast),
             out_shape=jax.ShapeDtypeStruct((1, rows, width), jnp.float32),
@@ -350,7 +352,7 @@
                 dma, dma, dma, dma, dma((slow,)), dma((slow,)), dma((slow,)), dma((3,)), dma((3,)),
             ],
             compiler_params=pltpu.CompilerParams(
-                collective_id=0, has_side_effects=True, vmem_limit_bytes=60 * 2**20),
+                collective_id=0, has_side_effects=True, vmem_limit_bytes=min(need + 12 * 2**20, 60 * 2**20)),
         )(logit_scale, logit_bias, subject_ids.reshape(n, rows), patch_rows)
 
     return jax.shard_map(

time: 46.9 us -> 47.4 us (1.011)
  local copies, waits for them, and re-layouts: 3.45 us -> 5.74 us
  Pallas kernels: 43.1 us -> 41.4 us
    unnamed x1 -> x7, local copies, waits for them, and re-layouts: 2.09 us -> 4.98 us
    pallas_call x1, Pallas kernels: 43.1 us -> 41.4 us  [on_device(): pl.pallas_call(functools.partial(kernel, n, fast), out_shape=jax.ShapeDty...]
    reshape x1, local copies, waits for them, and re-layouts: 1.36 us -> 0.77 us  [on_device(): subject_ids.reshape(n, rows)]
where the time goes in v4:
time: 47.4 us; the launch traced here: 47.2 us
  Pallas kernels  41.4 us (87%)
  local copies, waits for them, and re-layouts  5.74 us (12%)
    pallas_call x1, Pallas kernels, on_device(): pl.pallas_call(functools.partial(kernel, n, fast), out_shape=jax.ShapeDty...  41.4 us
    unnamed x7, local copies, waits for them, and re-layouts  4.98 us

profile of v4, /device:TPU:0, one launch (start us, length us, event | category | flops | bytes accessed | tf_op | source)
XLA Modules:
  0.0 47.2 jit_solution(14650529438020295550)
XLA Ops:
  0.0 0.8 %reshape.3.ids_ref = s32[8,192]{1,0:T(8,128)S(1)} reshape(s32[1536]{0:T(1024)} %param.5) | data formatting | bytes 12288 | tf_op jit(solution)/shard_map/reshape | solution.py:356
  0.8 0.0 copy-start
  0.8 2.8 %copy-done = bf16[1,192,16,1024]{3,2,1,0:T(8,128)(2,1)S(1)} copy-done((bf16[1,192,16,1024]{3,2,1,0:T(8,128)(2,1)S(1)}, bf16[1,192,16,1024]{3,2,1,0:T(8,128)(2,1)}, u32[]{:S(2)}) %copy-start) | copy-done | bytes 6291480
  3.6 0.0 copy-start.1
  3.6 0.7 %copy-done.1 = f32[2]{0:T(128)S(1)} copy-done((f32[2]{0:T(128)S(1)}, f32[2]{0:T(128)}, u32[]{:S(2)}) %copy-start.1) | copy-done | bytes 32
  4.2 0.0 copy-start.2
  4.2 0.7 %copy-done.2 = f32[2]{0:T(128)S(1)} copy-done((f32[2]{0:T(128)S(1)}, f32[2]{0:T(128)}, u32[]{:S(2)}) %copy-start.2) | copy-done | bytes 32
  4.9 41.4 %shard_map.46 = f32[1,192,1024]{2,1,0:T(8,128)S(1)} custom-call(f32[2]{0:T(128)S(1)} %copy-done.1, f32[2]{0:T(128)S(1)} %copy-done.2, s32[8,192]{1,0:T(8,128)S(1)} %reshape.3.ids_ref, bf16[1,192,16,1024]{3,2,1,0:T(8,128)(2,1)S(1)} %copy-done), custom_call_target="tpu_custom_call" | custom-call | tf_op jit(solution)/shard_map/pallas_call | solution.py:328
  46.3 0.9 %copy.6 = f32[1,192,1024]{2,1,0:T(8,128)} copy(f32[1,192,1024]{2,1,0:T(8,128)S(1)} %shard_map.46) | data formatting | bytes 1572864
Async XLA Ops:
  0.8 2.8 %copy-start = (bf16[1,192,16,1024]{3,2,1,0:T(8,128)(2,1)S(1)}, bf16[1,192,16,1024]{3,2,1,0:T(8,128)(2,1)}, u32[]{:S(2)}) copy-start(bf16[1,192,16,1024]{3,2,1,0:T(8,128)(2,1)} %x_ref.1) | copy-start | bytes 18874372
  3.6 0.7 %copy-start.1 = (f32[2]{0:T(128)S(1)}, f32[2]{0:T(128)}, u32[]{:S(2)}) copy-start(f32[2]{0:T(128)} %scale_ref.1) | copy-start | bytes 28
  4.2 0.7 %copy-start.2 = (f32[2]{0:T(128)S(1)}, f32[2]{0:T(128)}, u32[]{:S(2)}) copy-start(f32[2]{0:T(128)} %bias_ref.1) | copy-start | bytes 28
